TPU v7x, 32 devices: a whole 2x2x4 slice. The times are simulated.
32 devices in a mesh: groups: 2 (over y), blk: 4 (over z), cap: 2 (over x), yr: 2 (over core).
Axes of the slice: x: 2, y: 2, z: 4, core: 2. Of those that a mesh axis runs over, the one named last changes fastest.
Arguments:
- price: bfloat16 [16, 8, 64, 168], P(('groups', 'yr'), 'blk'), parts along dimension 0, may hold values from -0.5 to 0.5
- avail: bfloat16 [16, 8, 32, 168, 128], P(('groups', 'yr'), 'blk', 'cap'), parts along dimension 0, may hold values from 0 to 1
- tile_ids: int32 [16, 8, 32], P(('groups', 'yr'), 'blk', 'cap'), parts along dimension 0, may hold values from 0 to 255, as said below
- soc: bfloat16 [16, 8, 64, 4096], P(('groups', 'yr'), 'blk', None, 'cap'), parts along dimension 0, may hold values from -3 to 3
- link: bfloat16 [16, 8, 64, 4096], P(('groups', 'yr'), 'blk', None, 'cap'), parts along dimension 0, may hold values from -3 to 3
- retain: float32 [4096], P('cap'), may hold values from 0.3 to 1
- store_col: int32 [4096], P('cap'), may hold values from 0 to 32767, as said below
- weight: float32 [16, 8], P(('groups', 'yr'), 'blk'), parts along dimension 0, may hold values from 0.1 to 1
- capacity: float32 [65536], P('cap'), may hold values from 0.002 to 0.02
- objective: float32 [16, 8, 64], P(('groups', 'yr'), 'blk'), parts along dimension 0, may hold values from -6 to 6
Outputs:
- expected_cut: float32 [128, 2, 32768], P('groups', 'cap', ('blk', 'yr')), parts along dimension 0
- intercept: float32 [16, 8, 64], P(('groups', 'yr'), 'blk'), parts along dimension 0
There are 2 independent parts, one for each index of `groups`. A program takes and returns all parts, laid end to end along the dimension named above; an argument that names none is the same for every part. Nothing has to cross between parts.
Inputs may be any that keep to these rules, and one draw needn't show every extreme that they name: `tile_ids`: within one week and one capacity shard (entries k with equal k // 16) the tile indices are distinct. `store_col`: within one shard of 2048 storage units the columns are distinct.
All inputs are finite; a program needn't handle non-finite values.
Results may differ from a plain program's by a relative error of at most 0.0003.
Values may be sent and summed in bfloat16 or wider, within the bound.
A program may use at most 128 MiB of HBM per device.

v0:
```python
import jax
import jax.numpy as jnp
from jax import lax
from jax.sharding import PartitionSpec as P


def passed_along(value, axis, steps):
    count = lax.axis_size(axis)
    pairs = [(source, (source + steps) % count) for source in range(count)]
    return lax.ppermute(value, axis, pairs)


def local(price, avail, tile_ids, soc, link, retain, store_col, weight, capacity, objective):
    years_here, weeks_here, tiles_here, hours, width = avail.shape
    rows = price.shape[2]
    columns = capacity.shape[0]
    tile_count = columns // width
    first_week = link[:, :1]
    following = passed_along(first_week, "blk", -1)
    link_next = jnp.concatenate([link[:, 1:], following], axis=1)
    stor = (
        soc.astype(jnp.float32) + retain * link_next.astype(jnp.float32) - link.astype(jnp.float32)
    )
    gcut = jnp.einsum("ywrh,ywkhc->ywkrc", price, avail, preferred_element_type=jnp.float32)
    contrib = gcut * weight[:, :, None, None, None]
    contrib = jnp.transpose(contrib, (3, 0, 1, 2, 4)).reshape(
        rows, years_here * weeks_here * tiles_here, width
    )
    accum = jnp.zeros((rows, tile_count, width), jnp.float32)
    accum = accum.at[:, tile_ids.reshape(-1)].add(contrib).reshape(rows, columns)
    accum = accum.at[:, store_col].add(jnp.sum(weight[:, :, None, None] * stor, axis=(0, 1)))
    cap_tiles = capacity.reshape(tile_count, width)[tile_ids]
    partial_dots = jnp.sum(gcut * cap_tiles[:, :, :, None, :], axis=(2, 4))
    partial_dots = partial_dots + jnp.sum(stor * capacity[store_col], axis=-1)
    total_dots = lax.psum(partial_dots, "cap")
    intercept = objective - total_dots
    piece = lax.psum_scatter(accum, ("blk", "yr"), scatter_dimension=1, tiled=True)
    return (piece[:, None, :], intercept)


def solution(mesh):
    return jax.shard_map(
        local,
        mesh=mesh,
        in_specs=(
            P(("groups", "yr"), "blk", None, None),
            P(("groups", "yr"), "blk", "cap", None, None),
            P(("groups", "yr"), "blk", "cap"),
            P(("groups", "yr"), "blk", None, "cap"),
            P(("groups", "yr"), "blk", None, "cap"),
            P("cap"),
            P("cap"),
            P(("groups", "yr"), "blk"),
            P("cap"),
            P(("groups", "yr"), "blk", None),
        ),
        out_specs=(P("groups", "cap", ("blk", "yr")), P(("groups", "yr"), "blk", None)),
        check_vma=False,
    )
```

profile of v0, /device:TPU:0, one launch (start us, length us, event | category | flops | bytes accessed | tf_op | source)
XLA Modules:
  0.0 274.9 jit_solution(14836594615960332909)
XLA Ops:
  7.2 0.0 copy-start
  7.2 0.0 copy-start.3
  7.2 0.0 copy-start.7
  7.2 0.0 copy-start.5
  7.2 0.0 copy-start.1
  7.2 0.0 reduce-scatter.2.cloned.1.call-start
  7.3 2.8 %fusion.3 = (bf16[4,1,64,2048]{3,2,1,0:T(8,128)(2,1)S(1)}, bf16[4,1,64,2048]{3,2,1,0:T(8,128)(2,1)}) fusion(bf16[4,2,64,2048]{3,2,1,0:T(8,128)(2,1)} %param.14), kind=kLoop, calls=%fused_computation.18 | loop fusion | bytes 4194304 | tf_op jit(solution)/shard_map/slice | solution.py:20
  10.0 5.0 %collective-permute-start = (bf16[4,1,64,2048]{3,2,1,0:T(8,128)(2,1)}, bf16[4,1,64,2048]{3,2,1,0:T(8,128)(2,1)}, u32[]{:S(2)}, u32[]{:S(2)}) collective-permute-start(bf16[4,1,64,2048]{3,2,1,0:T(8,128)(2,1)} %get-tuple-element.13), channel_id=1, source_target_pairs={{0,12},{4,0},{8,4},{12,8},{1,13},{5,1},{9,5},{13,9},{2,14},{6,2},{... | collective-permute-start | bytes 3145736 | tf_op jit(solution)/shard_map/ppermute | solution.py:10
  15.1 0.0 copy-done.3
  15.1 0.1 reshape.49
  15.2 0.0 copy-done.7
  15.2 0.1 copy.20
  15.3 0.1 reshape.55
  15.4 0.0 copy-done.5
  15.4 0.0 copy-done.1
  15.4 11.8 %gather_fusion.1 = f32[2048]{0:T(1024)S(1)} fusion(f32[32768]{0:T(1024)S(1)} %copy-done.1, s32[2048]{0:T(1024)S(1)} %get-tuple-element.14), kind=kCustom, calls=%fused_computation.1 | custom fusion | bytes 24576 | tf_op jit(solution)/shard_map/gather | solution.py:34
  27.2 0.6 gather_fusion
  27.8 0.0 copy-done
  27.9 5.4 %multiply_reduce_fusion.1 = (f32[4,2,64]{2,1,0:T(2,128)S(1)}, f32[4,2,16,128,64]{3,4,2,1,0:T(8,128)}) fusion(f32[4,2,16,128]{3,2,1,0:T(8,128)S(1)} %bitcast.25, f32[4,2]{1,0:T(4,128)S(1)} %copy.20, bf16[4,2,16,168,128]{4,3,2,1,0:T(8,128)(2,1)} %param.11, bf16[4,2,64,168]{3,2,1,0:T(8,128)(2,1)S(1)} %copy-done), kind=kOutput, calls=%fused_computation.5 | convolution fusion | flops 355466752 | bytes 9938976 | tf_op jit(solution)/shard_map/ywrh,ywkhc->ywkrc/dot_general | solution.py:24
  33.2 4.3 %broadcast_in_dim.8 = f32[64,256,128]{2,0,1:T(8,128)} broadcast(f32[]{:T(128)} %constant.4.clone.1), dimensions={} | broadcast | bytes 8388612 | tf_op jit(solution)/shard_map/broadcast_in_dim | solution.py:29
  37.5 20.2 %scatter_fusion = f32[64,256,128]{2,0,1:T(8,128)} fusion(f32[64,256,128]{2,0,1:T(8,128)} %broadcast_in_dim.8, s32[128]{0:T(128)S(1)} %fusion.2, f32[128,64,128]{2,1,0:T(8,128)} %bitcast.22), kind=kCustom, calls=%fused_computation.2 | custom fusion | flops 1048576 | bytes 12583424 | tf_op jit(solution)/shard_map/scatter-add | solution.py:30
  57.7 0.0 copy-start.2
  57.7 0.0 copy-start.4
  57.7 12.4 %copy.27 = f32[64,256,128]{0,2,1:T(8,128)} copy(f32[64,256,128]{2,0,1:T(8,128)} %scatter_fusion) | data formatting | bytes 16777216 | tf_op jit(solution)/shard_map/reshape | solution.py:30
  70.1 0.0 collective-permute-done
  70.1 0.0 copy-done.2
  70.1 0.0 copy-done.4
  70.1 4.3 %multiply_reduce_fusion = (f32[4,2,64]{2,1,0:T(2,128)S(1)}, f32[64,2048]{1,0:T(8,128)}) fusion(bf16[4,2,64,2048]{3,2,1,0:T(8,128)(2,1)S(1)} %copy-done.2, bf16[4,2,64,2048]{3,2,1,0:T(8,128)(2,1)} %param.13, f32[2048]{0:T(1024)S(1)} %gather_fusion.1, f32[2048]{0:T(1024)S(1)} %copy-done.4, bf16[4,1,64,2048]{3,2,1,0:T(8,128)(2,1)} %collective-permute-done, ...), kind=kLoop, calls=%fused_computation.4 | loop fusion | flops 11402752 | bytes 6834208 | tf_op jit(solution)/shard_map/reduce_sum | solution.py:34
  74.4 1.4 copy.24
  75.8 21.8 %scatter_fusion.1 = f32[64,32768]{0,1:T(8,128)} fusion(f32[64,32768]{0,1:T(8,128)} %bitcast.21, s32[2048]{0:T(1024)S(1)} %get-tuple-element.15, f32[2048,64]{1,0:T(8,128)S(1)} %copy.24), kind=kCustom, calls=%fused_computation.3 | custom fusion | flops 131072 | bytes 1581056 | tf_op jit(solution)/shard_map/scatter-add | solution.py:31
  97.6 0.0 copy-start.6
  97.6 0.0 reduce-scatter.2.cloned.1.call-update
  97.6 4.9 %psum.7 = f32[4,2,64]{2,1,0:T(2,128)S(1)} all-reduce(f32[4,2,64]{2,1,0:T(2,128)S(1)} %add.43), channel_id=1, replica_groups=mesh['groups'=2,'blk'=4,'cap'=2,'yr'=2] {'cap'}, use_global_device_ids=true, to_apply=%region_6.0 | all-reduce | flops 512 | bytes 4096 | tf_op jit(solution)/shard_map/psum | solution.py:35
  102.5 0.0 copy-done.6
  102.5 0.6 sub.7
  103.1 161.0 %reduce-scatter.2.cloned.1.call-done = f32[64,4096]{0,1:T(8,128)} async-done(((f32[64,32768]{0,1:T(8,128)}), f32[64,4096]{0,1:T(8,128)}) %reduce-scatter.2.cloned.1.call-update) | async-done | bytes 1048592 | tf_op jit(solution)/shard_map/reduce_scatter | solution.py:37
  264.2 3.9 %copy.25 = f32[64,1,4096]{2,1,0:T(1,128)} copy(f32[64,1,4096]{0,2,1:T(8,128)} %bitcast.23) | data formatting | bytes 2097152
  (5 shorter events, 0.0 us)
Async XLA Ops:
  7.2 20.7 %copy-start = (bf16[4,2,64,168]{3,2,1,0:T(8,128)(2,1)S(1)}, bf16[4,2,64,168]{3,2,1,0:T(8,128)(2,1)}, u32[]{:S(2)}) copy-start(bf16[4,2,64,168]{3,2,1,0:T(8,128)(2,1)} %param.10) | copy-start | bytes 516100
  7.2 7.9 %copy-start.3 = (s32[4,2,16]{2,1,0:T(2,128)S(1)}, s32[4,2,16]{2,1,0:T(2,128)}, u32[]{:S(2)}) copy-start(s32[4,2,16]{2,1,0:T(2,128)} %param.12) | copy-start | bytes 1540
  7.2 8.0 %copy-start.7 = (f32[4,2]{0,1:T(2,128)S(1)}, f32[4,2]{0,1:T(2,128)}, u32[]{:S(2)}) copy-start(f32[4,2]{0,1:T(2,128)} %param.17) | copy-start | bytes 100
  7.2 8.2 %copy-start.5 = (s32[2048]{0:T(1024)S(1)}, s32[2048]{0:T(1024)}, u32[]{:S(2)}) copy-start(s32[2048]{0:T(1024)} %param.16) | copy-start | bytes 24580
  7.2 8.2 %copy-start.1 = (f32[32768]{0:T(1024)S(1)}, f32[32768]{0:T(1024)}, u32[]{:S(2)}) copy-start(f32[32768]{0:T(1024)} %param.18) | copy-start | bytes 393220
  7.2 256.9 %reduce-scatter.2.cloned.1.call-start = ((), (), s32[]{:S(2)}) async-start(), calls=%async_computation.1 | async-start | bytes 18874368 | tf_op jit(solution)/shard_map/reduce_scatter | solution.py:37
  10.0 60.1 %collective-permute-start = (bf16[4,1,64,2048]{3,2,1,0:T(8,128)(2,1)}, bf16[4,1,64,2048]{3,2,1,0:T(8,128)(2,1)}, u32[]{:S(2)}, u32[]{:S(2)}) collective-permute-start(bf16[4,1,64,2048]{3,2,1,0:T(8,128)(2,1)} %get-tuple-element.13), channel_id=1, source_target_pairs={{0,12},{4,0},{8,4},{12,8},{1,13},{5,1},{9,5},{13,9},{2,14},{6,2},{... | collective-permute-start | bytes 3145736 | tf_op jit(solution)/shard_map/ppermute | solution.py:10
  57.7 12.4 %copy-start.2 = (bf16[4,2,64,2048]{3,2,1,0:T(8,128)(2,1)S(1)}, bf16[4,2,64,2048]{3,2,1,0:T(8,128)(2,1)}, u32[]{:S(2)}) copy-start(bf16[4,2,64,2048]{3,2,1,0:T(8,128)(2,1)} %param.14) | copy-start | bytes 6291460
  57.7 12.4 %copy-start.4 = (f32[2048]{0:T(1024)S(1)}, f32[2048]{0:T(1024)}, u32[]{:S(2)}) copy-start(f32[2048]{0:T(1024)} %param.15) | copy-start | bytes 24580
  97.6 5.0 %copy-start.6 = (f32[4,2,64]{2,1,0:T(2,128)S(1)}, f32[4,2,64]{2,1,0:T(2,128)}, u32[]{:S(2)}) copy-start(f32[4,2,64]{2,1,0:T(2,128)} %param.19) | copy-start | bytes 6148
Sparse Core Ops, SparseCore 0:
  97.7 166.4 reduce-scatter.1
where the time goes:
time: 276 us; the launch traced here: 275 us
  waiting for transfers between devices  161 us (58%)
  other arithmetic  46.9 us (17%)
  local copies, waits for them, and re-layouts  37.4 us (14%)
  between operations  14.1 us (5%)
  matrix products  5.39 us (2%)
  starting transfers between devices  5.09 us (2%)
  blocking collectives  4.95 us (2%)
    reduce_scatter x1, waiting for transfers between devices, local(): lax.psum_scatter(accum, ('blk', 'yr'), scatter_dimension=1, tiled=True)  161 us
    scatter-add x1, other arithmetic, local(): accum.at[:, store_col]  21.8 us
    scatter-add x1, other arithmetic, local(): accum.at[:, tile_ids.reshape(-1)].add(contrib).reshape(rows, columns)  20.2 us
    reshape x1, local copies, waits for them, and re-layouts, local(): accum.at[:, tile_ids.reshape(-1)].add(contrib).reshape(rows, columns)  12.4 us
    gather x1, local copies, waits for them, and re-layouts, local(): partial_dots = partial_dots + jnp.sum(stor * capacity[store_col], axis=-1)  11.8 us
  transfers between devices with their start and end apart: 2, of which 1 were waited for; matrix products, arithmetic and copies ran while one was open for 20% of the time, Pallas kernels for 0%

commit v1 on v0

v1 whole, which is shorter than its diff:
```python
import functools

import jax
import jax.numpy as jnp
from jax import lax
from jax.experimental import pallas as pl
from jax.experimental.pallas import tpu as pltpu
from jax.sharding import PartitionSpec as P

MESH = pl.DeviceIdType.MESH
LANES = 128
VMEM_LIMIT = 48 * 1024 * 1024


def split3(value):
    hi = value.astype(jnp.bfloat16)
    rest = value - hi.astype(jnp.float32)
    mid = rest.astype(jnp.bfloat16)
    lo = (rest - mid.astype(jnp.float32)).astype(jnp.bfloat16)
    return hi, mid, lo


def local_kernel(
    years, weeks, ids_ref, weight_ref, price_ref, avail_ref, soc_ref, link_ref, retain_ref, col_ref, cap_ref,
    acc_ref, wsum_ref, d_ref, e_ref, caps_ref,
):
    step = pl.program_id(0)
    tiles = avail_ref.shape[2]
    rows = price_ref.shape[2]
    units = retain_ref.shape[1]
    tile_count = cap_ref.shape[0]

    @pl.when(step == 0)
    def _():
        def clear(i, carry):
            acc_ref[i] = jnp.zeros((rows, LANES), jnp.float32)
            return carry

        lax.fori_loop(0, tile_count, clear, 0)
        wsum_ref[...] = jnp.zeros_like(wsum_ref)
        d_ref[...] = jnp.zeros_like(d_ref)
        e_ref[...] = jnp.zeros_like(e_ref)
        turned = jnp.transpose(cap_ref[:, 0, :])
        parts = split3(turned)
        chunk = 512
        for first in range(0, units, chunk):
            col = col_ref[:, first:first + chunk]
            tile_of = lax.broadcasted_iota(jnp.int32, (tile_count, chunk), 0)
            pick = jnp.where(tile_of == (col >> 7), 1.0, 0.0).astype(jnp.bfloat16)
            found = jnp.zeros((LANES, chunk), jnp.float32)
            for part in parts:
                found += jnp.dot(part, pick, preferred_element_type=jnp.float32)
            lane_of = lax.broadcasted_iota(jnp.int32, (LANES, chunk), 0)
            found = jnp.where(lane_of == (col & 127), found, 0.0)
            caps_ref[:, first:first + chunk] = jnp.sum(found, axis=0, keepdims=True)

    here = weight_ref[step]
    inside = lax.rem(step, weeks)
    before = jnp.where(inside > 0, weight_ref[jnp.maximum(step - 1, 0)], 0.0)
    duals = price_ref[0, 0]
    tile_dots = jnp.zeros((rows, LANES), jnp.float32)
    for k in range(tiles):
        index = ids_ref[step * tiles + k]
        cut = jnp.dot(duals, avail_ref[0, 0, k], preferred_element_type=jnp.float32)
        tile_dots += cut * cap_ref[index]
        acc_ref[index] += here * cut

    lane = lax.broadcasted_iota(jnp.int32, (16, LANES), 1)
    last = (step // weeks) * weeks + weeks - 1
    d_ref[...] += jnp.where(
        lax.broadcasted_iota(jnp.int32, (rows, LANES), 1) == step, jnp.sum(tile_dots, axis=1, keepdims=True), 0.0
    )

    def band(i, carry):
        at = pl.ds(pl.multiple_of(i * 16, 16), 16)
        dots = jnp.zeros((16, LANES), jnp.float32)
        nexts = jnp.zeros((16, LANES), jnp.float32)
        for first in range(0, units, LANES):
            span = slice(first, first + LANES)
            s = soc_ref[0, 0, at, span].astype(jnp.float32)
            l = link_ref[0, 0, at, span].astype(jnp.float32)
            kept = retain_ref[:, span] * l
            flow = s - l
            worth = caps_ref[:, span]
            wsum_ref[at, span] += here * flow + before * kept
            dots += worth * flow
            nexts += worth * kept
        own = jnp.sum(dots, axis=1, keepdims=True)
        later = jnp.sum(nexts, axis=1, keepdims=True)
        d_ref[at, :] += jnp.where(lane == step, own, 0.0) + jnp.where((lane == step - 1) & (inside > 0), later, 0.0)
        e_ref[at, :] += jnp.where((lane == last) & (inside == 0), later, 0.0)
        return carry

    lax.fori_loop(0, rows // 16, band, 0)


def code(x):
    top = jnp.maximum(jnp.max(jnp.abs(x), axis=0, keepdims=True), 1e-30)
    q = jnp.round(x * (32767.0 / top)).astype(jnp.int32).astype(jnp.int16)
    return q, top * (1.0 / 32767.0)


def value_of(q, scale):
    return q.astype(jnp.int32).astype(jnp.float32) * scale


def reduce_kernel(
    nb, nc, acc_ref, wsum_ref, first_ref, retain_ref, tail_ref, d_ref, e_ref, col_ref, objective_ref,
    out_ref, intercept_ref,
    pair, q_out, s_out, q_in, s_in, tail_in, d_in, e_in, w_own, w_pair, wq_out, ws_out, wq_in, ws_in, w_tot, w_hl,
    onel, placed,
    pair_sem, q_sem, s_sem, tail_sem, d_sem, e_sem, wp_sem, wq_sem, ws_sem, wt_sem,
):
    b, c, u = lax.axis_index("blk"), lax.axis_index("cap"), lax.axis_index("yr")
    sib = 1 - u
    ahead, behind = lax.rem(b + 1, nb), lax.rem(b + nb - 1, nb)
    per = out_ref.shape[1] // LANES
    rows, units = wsum_ref.shape
    half = units // 2
    years = first_ref.shape[0]
    order = list(range(nb - 1, 0, -1))
    power = nb & (nb - 1) == 0

    def target(d):
        return b ^ d if power else lax.rem(b + d, nb)

    def source(d):
        return b ^ d if power else lax.rem(b + nb - d, nb)

    barrier = pltpu.get_barrier_semaphore()
    pl.semaphore_signal(barrier, inc=1, device_id={"yr": sib}, device_id_type=MESH)
    for d in order:
        pl.semaphore_signal(barrier, inc=1, device_id={"blk": source(d)}, device_id_type=MESH)
    for dc in range(1, nc):
        other = lax.rem(c + dc, nc)
        pl.semaphore_signal(barrier, inc=1, device_id={"cap": other}, device_id_type=MESH)
        pl.semaphore_signal(barrier, inc=1, device_id={"blk": ahead, "cap": other}, device_id_type=MESH)
    pl.semaphore_wait(barrier, 1 + (nb - 1) + 2 * (nc - 1))

    def remote(src, dst, sem, device):
        return pltpu.make_async_remote_copy(
            src_ref=src, dst_ref=dst, send_sem=sem.at[0], recv_sem=sem.at[1], device_id=device, device_id_type=MESH
        )

    tail_copy = remote(tail_ref, tail_in, tail_sem, {"blk": ahead})
    tail_copy.start()
    pair_copies = []
    for j, d in enumerate(order + [0]):
        start = pl.multiple_of((2 * target(d) + sib) * per, per)
        pair_copies.append(remote(acc_ref.at[pl.ds(start, per)], pair.at[j], pair_sem.at[j], {"yr": sib}))
    pair_copies[0].start()
    small = []
    for dc in range(1, nc):
        other = lax.rem(c + dc, nc)
        small.append(remote(d_ref, d_in.at[dc - 1], d_sem.at[dc - 1], {"cap": other}))
    for dc in range(nc):
        other = lax.rem(c + dc, nc)
        small.append(remote(e_ref, e_in.at[dc], e_sem.at[dc], {"blk": behind, "cap": other}))
    for copy in small:
        copy.start()

    tail_copy.wait()
    for h in range(2):
        for first in range(0, half, LANES):
            span = slice(h * half + first, h * half + first + LANES)

            def band(i, carry, h=h, first=first, span=span):
                at = pl.ds(pl.multiple_of(i * 16, 16), 16)
                total = jnp.zeros((16, LANES), jnp.float32)
                for y in range(years):
                    total += tail_in[y] * first_ref[y, 0, at, span].astype(jnp.float32)
                w_own[h, at, first:first + LANES] = wsum_ref[at, span] + retain_ref[:, span] * total
                return carry

            lax.fori_loop(0, rows // 16, band, 0)
    w_copy = remote(w_own.at[sib], w_pair, wp_sem, {"yr": sib})
    w_copy.start()
    for copy in pair_copies[1:]:
        copy.start()

    def send_piece(j):
        d = order[j]
        base = (2 * target(d) + u) * per

        def one(i, carry):
            q, s = code(acc_ref[base + i] + pair[j, i])
            q_out[j, i] = q
            s_out[j, pl.ds(i, 1)] = s
            return carry

        pair_copies[j].wait()
        lax.fori_loop(0, per, one, 0)
        copies = [
            remote(q_out.at[j], q_in.at[j], q_sem.at[j], {"blk": target(d)}),
            remote(s_out.at[j], s_in.at[j], s_sem.at[j], {"blk": target(d)}),
        ]
        for copy in copies:
            copy.start()
        return copies

    w_copy.wait()
    for first in range(0, half, LANES):
        span = slice(first, first + LANES)
        total = w_own[u, :, span] + w_pair[:, span]
        q, s = code(total)
        w_tot[u, :, span] = total
        wq_out[:, span] = q
        ws_out[:, span] = s
    w_copies = []
    for j, d in enumerate(order):
        w_copies.append(remote(wq_out, wq_in.at[j], wq_sem.at[j], {"blk": target(d)}))
        w_copies.append(remote(ws_out, ws_in.at[j], ws_sem.at[j], {"blk": target(d)}))
    for copy in w_copies:
        copy.start()

    sent = []
    for j in range(len(order)):
        sent.append(send_piece(j))

    for copy in w_copies:
        copy.wait()
    for first in range(0, half, LANES):
        span = slice(first, first + LANES)
        total = w_tot[u, :, span]
        for j in range(len(order)):
            total += value_of(wq_in[j, :, span], ws_in[j, :, span])
        w_tot[u, :, span] = total
    t_copy = remote(w_tot.at[u], w_tot.at[u], wt_sem, {"yr": sib})
    t_copy.start()
    chunk = 256
    for first in range(0, units, chunk):
        lane_of = lax.broadcasted_iota(jnp.int32, (LANES, chunk), 0)
        hot = jnp.where(lane_of == (col_ref[:, first:first + chunk] & 127), 1.0, 0.0)
        onel[first:first + chunk, :] = jnp.transpose(hot).astype(jnp.bfloat16)
    t_copy.wait()
    for h in range(2):
        total = w_tot[h]
        hi = total.astype(jnp.bfloat16)
        w_hl[:rows, h * half:(h + 1) * half] = hi
        w_hl[rows:, h * half:(h + 1) * half] = (total - hi.astype(jnp.float32)).astype(jnp.bfloat16)
    mine = (2 * b + u) * per

    def place(i, carry):
        mask = jnp.where((col_ref[...] >> 7) == mine + i, 1.0, 0.0).astype(jnp.bfloat16)
        both = jnp.dot(w_hl[...] * mask, onel[...], preferred_element_type=jnp.float32)
        placed[i] = both[:rows] + both[rows:]
        return carry

    lax.fori_loop(0, per, place, 0)

    pair_copies[-1].wait()
    for copies in sent:
        for copy in copies:
            copy.wait()

    def finish(i, carry):
        total = acc_ref[mine + i] + pair[nb - 1, i] + placed[i]
        for j in range(len(order)):
            total += value_of(q_in[j, i], s_in[j, pl.ds(i, 1)])
        out_ref[:, pl.ds(pl.multiple_of(i * LANES, LANES), LANES)] = total
        return carry

    lax.fori_loop(0, per, finish, 0)

    for copy in small:
        copy.wait()
    dots = d_ref[...]
    for dc in range(1, nc):
        dots += d_in[dc - 1]
    for dc in range(nc):
        dots += e_in[dc]
    intercept_ref[...] = objective_ref[...] - jnp.transpose(dots)[:objective_ref.shape[0], :]


def local(nb, nc, price, avail, tile_ids, soc, link, retain, store_col, weight, capacity, objective):
    years, weeks, tiles, hours, width = avail.shape
    rows, units = soc.shape[2:]
    columns = capacity.shape[0]
    tile_count = columns // width
    steps = years * weeks
    piece = columns // (2 * nb)
    per = piece // width
    half = units // 2
    retain2 = retain.reshape(1, units)
    col2 = store_col.reshape(1, units)
    f32 = jnp.float32

    def week(g, *_):
        return (g // weeks, lax.rem(g, weeks), 0, 0)

    def fixed(rank):
        return lambda g, *_: (0,) * rank

    acc, wsum, d, e = pl.pallas_call(
        functools.partial(local_kernel, years, weeks),
        grid_spec=pltpu.PrefetchScalarGridSpec(
            num_scalar_prefetch=2,
            grid=(steps,),
            in_specs=[
                pl.BlockSpec((1, 1, rows, hours), week),
                pl.BlockSpec((1, 1, tiles, hours, width), lambda g, *_: (g // weeks, lax.rem(g, weeks), 0, 0, 0)),
                pl.BlockSpec((1, 1, rows, units), week),
                pl.BlockSpec((1, 1, rows, units), week),
                pl.BlockSpec((1, units), fixed(2)),
                pl.BlockSpec((1, units), fixed(2)),
                pl.BlockSpec((tile_count, 1, width), fixed(3)),
            ],
            out_specs=[
                pl.BlockSpec((tile_count, rows, width), fixed(3)),
                pl.BlockSpec((rows, units), fixed(2)),
                pl.BlockSpec((rows, LANES), fixed(2)),
                pl.BlockSpec((rows, LANES), fixed(2)),
            ],
            scratch_shapes=[pltpu.VMEM((1, units), f32)],
        ),
        out_shape=[
            jax.ShapeDtypeStruct((tile_count, rows, width), f32),
            jax.ShapeDtypeStruct((rows, units), f32),
            jax.ShapeDtypeStruct((rows, LANES), f32),
            jax.ShapeDtypeStruct((rows, LANES), f32),
        ],
        compiler_params=pltpu.CompilerParams(vmem_limit_bytes=VMEM_LIMIT),
    )(tile_ids.reshape(-1), weight.reshape(-1), price, avail, soc, link, retain2, col2, capacity.reshape(tile_count, 1, width))

    tail = jnp.broadcast_to(weight[:, weeks - 1][:, None, None], (years, 1, LANES))
    vmem = pl.BlockSpec(memory_space=pltpu.VMEM)
    dma = pltpu.SemaphoreType.DMA
    out, intercept = pl.pallas_call(
        functools.partial(reduce_kernel, nb, nc),
        grid=(1,),
        in_specs=[vmem, vmem, pl.BlockSpec((years, 1, rows, units), lambda g: (0, 0, 0, 0))] + [vmem] * 6,
        out_specs=[vmem, vmem],
        out_shape=[
            jax.ShapeDtypeStruct((rows, piece), f32),
            jax.ShapeDtypeStruct((steps, rows), f32),
        ],
        scratch_shapes=[
            pltpu.VMEM((nb, per, rows, width), f32),
            pltpu.VMEM((nb - 1, per, rows, width), jnp.int16),
            pltpu.VMEM((nb - 1, per, width), f32),
            pltpu.VMEM((nb - 1, per, rows, width), jnp.int16),
            pltpu.VMEM((nb - 1, per, width), f32),
            pltpu.VMEM((years, 1, LANES), f32),
            pltpu.VMEM((max(nc - 1, 1), rows, LANES), f32),
            pltpu.VMEM((nc, rows, LANES), f32),
            pltpu.VMEM((2, rows, half), f32),
            pltpu.VMEM((rows, half), f32),
            pltpu.VMEM((rows, half), jnp.int16),
            pltpu.VMEM((1, half), f32),
            pltpu.VMEM((nb - 1, rows, half), jnp.int16),
            pltpu.VMEM((nb - 1, 1, half), f32),
            pltpu.VMEM((2, rows, half), f32),
            pltpu.VMEM((2 * rows, units), jnp.bfloat16),
            pltpu.VMEM((units, LANES), jnp.bfloat16),
            pltpu.VMEM((per, rows, width), f32),
            dma((nb, 2)),
            dma((nb - 1, 2)),
            dma((nb - 1, 2)),
            dma((2,)),
            dma((max(nc - 1, 1), 2)),
            dma((nc, 2)),
            dma((2,)),
            dma((nb - 1, 2)),
            dma((nb - 1, 2)),
            dma((2,)),
        ],
        compiler_params=pltpu.CompilerParams(
            collective_id=0, has_side_effects=True, vmem_limit_bytes=VMEM_LIMIT
        ),
    )(acc, wsum, link, retain2, tail, d, e, col2, objective.reshape(steps, rows))
    return (out[:, None, :], intercept.reshape(years, weeks, rows))


def solution(mesh):
    return jax.shard_map(
        functools.partial(local, mesh.shape["blk"], mesh.shape["cap"]),
        mesh=mesh,
        in_specs=(
            P(("groups", "yr"), "blk", None, None),
            P(("groups", "yr"), "blk", "cap", None, None),
            P(("groups", "yr"), "blk", "cap"),
            P(("groups", "yr"), "blk", None, "cap"),
            P(("groups", "yr"), "blk", None, "cap"),
            P("cap"),
            P("cap"),
            P(("groups", "yr"), "blk"),
            P("cap"),
            P(("groups", "yr"), "blk", None),
        ),
        out_specs=(P("groups", "cap", ("blk", "yr")), P(("groups", "yr"), "blk", None)),
        check_vma=False,
    )
```

time: 276 us -> 103 us (0.37)
  waiting for transfers between devices: 161 us -> 0 us
  Pallas kernels: 0 us -> 89.9 us
  other arithmetic: 46.9 us -> 0 us
  local copies, waits for them, and re-layouts: 37.4 us -> 11.5 us
  between operations: 14.1 us -> 0.66 us
  matrix products: 5.39 us -> 0 us
  starting transfers between devices: 5.09 us -> 0 us
  blocking collectives: 4.95 us -> 0 us
    reduce_scatter x1 -> x0, waiting for transfers between devices: 161 us -> none  [local(): lax.psum_scatter(accum, ('blk', 'yr'), scatter_dimension=1, tiled=True)]
    pallas_call x0 -> x2, Pallas kernels: none -> 89.9 us  [the longest x1 74.4 us: local(): pl.pallas_call(functools.partial(reduce_kernel, nb, nc), grid=(1,), in_sp...]
    scatter-add x2 -> x0, other arithmetic: 42 us -> none  [the longest x1 21.8 us: local(): accum.at[:, store_col]]
    gather x2 -> x0, local copies, waits for them, and re-layouts: 12.4 us -> none  [the longest x1 11.8 us: local(): partial_dots = partial_dots + jnp.sum(stor * capacity[store_col], axis=-1)]
    reshape x1, local copies, waits for them, and re-layouts: 12.4 us -> 0.08 us  [local(): weight.reshape(-1)]
    unnamed x18 -> x19, local copies, waits for them, and re-layouts: 4.02 us -> 9.84 us
    dot_general x1 -> x0, matrix products: 5.39 us -> none  [local(): jnp.einsum('ywrh,ywkhc->ywkrc', price, avail, preferred_element_type=jnp....]
    ppermute x1 -> x0, starting transfers between devices: 5.05 us -> none  [passed_along(): return lax.ppermute(value, axis, pairs)]
  transfers between devices with their start and end apart: 2 -> 0, of which waited for: 1 -> 0; matrix products, arithmetic and copies ran while one was open for 20% -> 0% of each run, Pallas kernels for 0% -> 0%
where the time goes in v1:
time: 103 us; the launch traced here: 102 us
  Pallas kernels  89.9 us (87%)
  local copies, waits for them, and re-layouts  11.5 us (11%)
    pallas_call x1, Pallas kernels, local(): pl.pallas_call(functools.partial(reduce_kernel, nb, nc), grid=(1,), in_sp...  74.4 us
    pallas_call x1, Pallas kernels, local(): pl.pallas_call(functools.partial(local_kernel, years, weeks), grid_spec=p...  15.5 us
    unnamed x19, local copies, waits for them, and re-layouts  9.84 us

profile of v1, /device:TPU:0, one launch (start us, length us, event | category | flops | bytes accessed | tf_op | source)
XLA Modules:
  0.0 102.0 jit_solution(7725833349678177002)
XLA Ops:
  0.6 0.0 copy-start.7
  0.6 0.8 reshape.28.ids_ref
  1.4 0.7 slice_bitcast_fusion
  2.1 0.1 broadcast_in_dim.11.tail_ref
  2.2 0.8 copy.14
  2.9 0.1 reshape.29.weight_ref
  3.0 0.0 copy-start
  3.0 1.6 %copy-done = bf16[4,2,64,2048]{3,2,1,0:T(8,128)(2,1)S(1)} copy-done((bf16[4,2,64,2048]{3,2,1,0:T(8,128)(2,1)S(1)}, bf16[4,2,64,2048]{3,2,1,0:T(8,128)(2,1)}, u32[]{:S(2)}) %copy-start) | copy-done | bytes 2097176
  4.6 0.0 copy-start.2
  4.6 1.6 %copy-done.2 = bf16[4,2,64,2048]{3,2,1,0:T(8,128)(2,1)S(1)} copy-done((bf16[4,2,64,2048]{3,2,1,0:T(8,128)(2,1)S(1)}, bf16[4,2,64,2048]{3,2,1,0:T(8,128)(2,1)}, u32[]{:S(2)}) %copy-start.2) | copy-done | bytes 2097176
  6.2 0.0 copy-start.3
  6.2 0.9 copy-done.3
  7.2 0.0 copy-start.4
  7.2 0.9 copy-done.4
  8.1 0.0 copy-start.5
  8.1 0.7 copy-done.5
  8.8 0.0 copy-start.6
  8.8 0.7 copy-done.6
  9.5 0.0 copy-start.1
  9.5 15.5 %shard_map.113 = (f32[256,64,128]{2,1,0:T(8,128)}, f32[64,2048]{1,0:T(8,128)S(1)}, f32[64,128]{1,0:T(8,128)S(1)}, f32[64,128]{1,0:T(8,128)S(1)}) custom-call(s32[128]{0:T(128)S(1)} %reshape.28.ids_ref, f32[8]{0:T(128)S(1)} %reshape.29.weight_ref, bf16[4,2,64,168]{3,2,1,0:T(8,128)(2,1)S(1)} %copy-done.3, bf16[4,2,16,168,128]{4,3,2,1,0:T(8,128)(2,1)} %avail_ref.1, ...), custom_call_target="tpu_custom_call" | custom-call | tf_op jit(solution)/shard_map/pallas_call | solution.py:294
  25.0 0.0 copy-done.7
  25.0 0.0 copy-done.1
  25.0 74.4 %shard_map.114 = (f32[64,4096]{1,0:T(8,128)S(1)}, f32[8,64]{1,0:T(8,128)S(1)}) custom-call(f32[256,64,128]{2,1,0:T(8,128)} %get-tuple-element.8.acc_ref, f32[64,2048]{1,0:T(8,128)S(1)} %get-tuple-element.9.wsum_ref, bf16[4,2,64,2048]{3,2,1,0:T(8,128)(2,1)S(1)} %copy-done.1, f32[1,2048]{1,0:T(1,128)S(1)} %bitcast.11, ...), custom_call_target="tpu_custom_call" | custom-call | tf_op jit(solution)/shard_map/pallas_call | solution.py:328
  99.4 2.0 %copy.15 = f32[64,1,4096]{2,1,0:T(1,128)} copy(f32[64,1,4096]{2,0,1:T(8,128)S(1)} %bitcast.8) | data formatting | bytes 2097152
  101.4 0.6 copy.17
Async XLA Ops:
  0.6 24.3 %copy-start.7 = (f32[4,2,64]{2,1,0:T(2,128)S(1)}, f32[4,2,64]{2,1,0:T(2,128)}, u32[]{:S(2)}) copy-start(f32[4,2,64]{2,1,0:T(2,128)} %param.19) | copy-start | bytes 6148
  3.0 1.6 %copy-start = (bf16[4,2,64,2048]{3,2,1,0:T(8,128)(2,1)S(1)}, bf16[4,2,64,2048]{3,2,1,0:T(8,128)(2,1)}, u32[]{:S(2)}) copy-start(bf16[4,2,64,2048]{3,2,1,0:T(8,128)(2,1)} %first_ref.1) | copy-start | bytes 6291460
  4.6 1.6 %copy-start.2 = (bf16[4,2,64,2048]{3,2,1,0:T(8,128)(2,1)S(1)}, bf16[4,2,64,2048]{3,2,1,0:T(8,128)(2,1)}, u32[]{:S(2)}) copy-start(bf16[4,2,64,2048]{3,2,1,0:T(8,128)(2,1)} %soc_ref.1) | copy-start | bytes 6291460
  6.2 0.9 copy-start.3
  7.2 0.9 copy-start.4
  8.1 0.7 copy-start.5
  8.8 0.7 copy-start.6
  9.5 15.5 %copy-start.1 = (bf16[4,2,64,2048]{3,2,1,0:T(8,128)(2,1)S(1)}, bf16[4,2,64,2048]{3,2,1,0:T(8,128)(2,1)}, u32[]{:S(2)}) copy-start(bf16[4,2,64,2048]{3,2,1,0:T(8,128)(2,1)} %first_ref.1) | copy-start | bytes 6291460

commit v2 on v1

--- a/solution.py
+++ b/solution.py
@@ -9,7 +9,7 @@
 
 MESH = pl.DeviceIdType.MESH
 LANES = 128
-VMEM_LIMIT = 48 * 1024 * 1024
+VMEM_LIMIT = 60 * 1024 * 1024
 
 
 def split3(value):
@@ -105,11 +105,11 @@
 
 
 def reduce_kernel(
-    nb, nc, acc_ref, wsum_ref, first_ref, retain_ref, tail_ref, d_ref, e_ref, col_ref, objective_ref,
+    nb, nc, subs, acc_ref, wsum_ref, first_ref, retain_ref, tail_ref, d_ref, e_ref, col_ref, objective_ref,
     out_ref, intercept_ref,
-    pair, q_out, s_out, q_in, s_in, tail_in, d_in, e_in, w_own, w_pair, wq_out, ws_out, wq_in, ws_in, w_tot, w_hl,
-    onel, placed,
-    pair_sem, q_sem, s_sem, tail_sem, d_sem, e_sem, wp_sem, wq_sem, ws_sem, wt_sem,
+    mine, pair, q_out, s_out, q_in, s_in, tail_in, d_in, e_in, w_own, w_pair, wq_out, ws_out, wq_in, ws_in, w_tot,
+    w_hl, onel, placed,
+    mine_sem, pair_sem, q_sem, s_sem, tail_sem, d_sem, e_sem, wp_sem, wq_sem, ws_sem, wt_sem,
 ):
     b, c, u = lax.axis_index("blk"), lax.axis_index("cap"), lax.axis_index("yr")
     sib = 1 - u
@@ -118,24 +118,27 @@
     rows, units = wsum_ref.shape
     half = units // 2
     years = first_ref.shape[0]
-    order = list(range(nb - 1, 0, -1))
-    power = nb & (nb - 1) == 0
-
-    def target(d):
-        return b ^ d if power else lax.rem(b + d, nb)
-
-    def source(d):
-        return b ^ d if power else lax.rem(b + nb - d, nb)
+    share = per // subs
+    sequence = []
+    for k in range(nb):
+        for t in (nb - 1 - k, k):
+            if t not in sequence:
+                sequence.append(t)
 
     barrier = pltpu.get_barrier_semaphore()
     pl.semaphore_signal(barrier, inc=1, device_id={"yr": sib}, device_id_type=MESH)
-    for d in order:
-        pl.semaphore_signal(barrier, inc=1, device_id={"blk": source(d)}, device_id_type=MESH)
+    pl.semaphore_signal(barrier, inc=1, device_id={"blk": ahead}, device_id_type=MESH)
+    pl.semaphore_signal(barrier, inc=1, device_id={"blk": behind}, device_id_type=MESH)
     for dc in range(1, nc):
         other = lax.rem(c + dc, nc)
         pl.semaphore_signal(barrier, inc=1, device_id={"cap": other}, device_id_type=MESH)
         pl.semaphore_signal(barrier, inc=1, device_id={"blk": ahead, "cap": other}, device_id_type=MESH)
-    pl.semaphore_wait(barrier, 1 + (nb - 1) + 2 * (nc - 1))
+    local_copies = {}
+    for t in sequence:
+        start = pl.multiple_of((2 * t + u) * per, per)
+        local_copies[t] = pltpu.make_async_copy(acc_ref.at[pl.ds(start, per)], mine.at[t], mine_sem.at[t])
+        local_copies[t].start()
+    pl.semaphore_wait(barrier, 3 + 2 * (nc - 1))
 
     def remote(src, dst, sem, device):
         return pltpu.make_async_remote_copy(
@@ -144,11 +147,30 @@
 
     tail_copy = remote(tail_ref, tail_in, tail_sem, {"blk": ahead})
     tail_copy.start()
-    pair_copies = []
-    for j, d in enumerate(order + [0]):
-        start = pl.multiple_of((2 * target(d) + sib) * per, per)
-        pair_copies.append(remote(acc_ref.at[pl.ds(start, per)], pair.at[j], pair_sem.at[j], {"yr": sib}))
-    pair_copies[0].start()
+    pair_copies = {}
+    for t in sequence:
+        start = pl.multiple_of((2 * t + sib) * per, per)
+        pair_copies[t] = remote(acc_ref.at[pl.ds(start, per)], pair.at[t], pair_sem.at[t], {"yr": sib})
+    pair_copies[sequence[0]].start()
+
+    tail_copy.wait()
+    for h in range(2):
+        for first in range(0, half, LANES):
+            span = slice(h * half + first, h * half + first + LANES)
+
+            def band(i, carry, h=h, first=first, span=span):
+                at = pl.ds(pl.multiple_of(i * 16, 16), 16)
+                total = jnp.zeros((16, LANES), jnp.float32)
+                for y in range(years):
+                    total += tail_in[y] * first_ref[y, 0, at, span].astype(jnp.float32)
+                w_own[h, at, first:first + LANES] = wsum_ref[at, span] + retain_ref[:, span] * total
+                return carry
+
+            lax.fori_loop(0, rows // 16, band, 0)
+    w_copy = remote(w_own.at[sib], w_pair, wp_sem, {"yr": sib})
+    w_copy.start()
+    for t in sequence[1:]:
+        pair_copies[t].start()
     small = []
     for dc in range(1, nc):
         other = lax.rem(c + dc, nc)
@@ -159,108 +181,154 @@
     for copy in small:
         copy.start()
 
-    tail_copy.wait()
-    for h in range(2):
+    toward = (ahead, behind)
+    starts = (b == 0, b == nb - 1)
+    ends = (b == nb - 1, b == 0)
+
+    def store_copies(way):
+        return (
+            remote(wq_out.at[way], wq_in.at[way], wq_sem.at[way], {"blk": toward[way]}),
+            remote(ws_out.at[way], ws_in.at[way], ws_sem.at[way], {"blk": toward[way]}),
+        )
+
+    def store_send(way, add):
+        copies = store_copies(way)
+        if add:
+            for copy in copies:
+                copy.wait_recv()
         for first in range(0, half, LANES):
-            span = slice(h * half + first, h * half + first + LANES)
-
-            def band(i, carry, h=h, first=first, span=span):
-                at = pl.ds(pl.multiple_of(i * 16, 16), 16)
-                total = jnp.zeros((16, LANES), jnp.float32)
-                for y in range(years):
-                    total += tail_in[y] * first_ref[y, 0, at, span].astype(jnp.float32)
-                w_own[h, at, first:first + LANES] = wsum_ref[at, span] + retain_ref[:, span] * total
-                return carry
-
-            lax.fori_loop(0, rows // 16, band, 0)
-    w_copy = remote(w_own.at[sib], w_pair, wp_sem, {"yr": sib})
-    w_copy.start()
-    for copy in pair_copies[1:]:
-        copy.start()
-
-    def send_piece(j):
-        d = order[j]
-        base = (2 * target(d) + u) * per
-
-        def one(i, carry):
-            q, s = code(acc_ref[base + i] + pair[j, i])
-            q_out[j, i] = q
-            s_out[j, pl.ds(i, 1)] = s
-            return carry
-
-        pair_copies[j].wait()
-        lax.fori_loop(0, per, one, 0)
-        copies = [
-            remote(q_out.at[j], q_in.at[j], q_sem.at[j], {"blk": target(d)}),
-            remote(s_out.at[j], s_in.at[j], s_sem.at[j], {"blk": target(d)}),
-        ]
+            span = slice(first, first + LANES)
+            total = w_tot[u, :, span]
+            if add:
+                total += value_of(wq_in[way, :, span], ws_in[way, :, span])
+            q, s = code(total)
+            wq_out[way, :, span] = q
+            ws_out[way, :, span] = s
         for copy in copies:
             copy.start()
-        return copies
 
     w_copy.wait()
     for first in range(0, half, LANES):
         span = slice(first, first + LANES)
-        total = w_own[u, :, span] + w_pair[:, span]
-        q, s = code(total)
-        w_tot[u, :, span] = total
-        wq_out[:, span] = q
-        ws_out[:, span] = s
-    w_copies = []
-    for j, d in enumerate(order):
-        w_copies.append(remote(wq_out, wq_in.at[j], wq_sem.at[j], {"blk": target(d)}))
-        w_copies.append(remote(ws_out, ws_in.at[j], ws_sem.at[j], {"blk": target(d)}))
-    for copy in w_copies:
-        copy.start()
-
-    sent = []
-    for j in range(len(order)):
-        sent.append(send_piece(j))
-
-    for copy in w_copies:
-        copy.wait()
-    for first in range(0, half, LANES):
-        span = slice(first, first + LANES)
-        total = w_tot[u, :, span]
-        for j in range(len(order)):
-            total += value_of(wq_in[j, :, span], ws_in[j, :, span])
-        w_tot[u, :, span] = total
-    t_copy = remote(w_tot.at[u], w_tot.at[u], wt_sem, {"yr": sib})
-    t_copy.start()
-    chunk = 256
-    for first in range(0, units, chunk):
-        lane_of = lax.broadcasted_iota(jnp.int32, (LANES, chunk), 0)
-        hot = jnp.where(lane_of == (col_ref[:, first:first + chunk] & 127), 1.0, 0.0)
-        onel[first:first + chunk, :] = jnp.transpose(hot).astype(jnp.bfloat16)
-    t_copy.wait()
-    for h in range(2):
-        total = w_tot[h]
-        hi = total.astype(jnp.bfloat16)
-        w_hl[:rows, h * half:(h + 1) * half] = hi
-        w_hl[rows:, h * half:(h + 1) * half] = (total - hi.astype(jnp.float32)).astype(jnp.bfloat16)
-    mine = (2 * b + u) * per
+        w_tot[u, :, span] = w_own[u, :, span] + w_pair[:, span]
+    for way in range(2):
+        pl.when(starts[way])(functools.partial(store_send, way, False))
+    for way in range(2):
+        pl.when(jnp.logical_not(starts[way] | ends[way]))(functools.partial(store_send, way, True))
+
+    def piece_copies(way, t, n):
+        at = pl.ds(n * share, share)
+        return (
+            remote(q_out.at[t, at], q_in.at[way, t, at], q_sem.at[way, t, n], {"blk": toward[way]}),
+            remote(s_out.at[t, n], s_in.at[way, t, n], s_sem.at[way, t, n], {"blk": toward[way]}),
+        )
+
+    def piece_send(way, t, n, add):
+        copies = piece_copies(way, t, n)
+        if add:
+            for copy in copies:
+                copy.wait_recv()
+
+        def one(i, carry):
+            at = n * share + i
+            x = mine[t, at] + pair[t, at]
+            if add:
+                x += value_of(q_in[way, t, at], s_in[way, t, n, pl.ds(i, 1)])
+            q, s = code(x)
+            q_out[t, at] = q
+            s_out[t, n, pl.ds(i, 1)] = s
+            return carry
+
+        lax.fori_loop(0, share, one, 0)
+        for copy in copies:
+            copy.start()
+
+    def passes(way, t):
+        return (b < t) if way == 0 else (b > t)
+
+    def collect():
+        for way in range(2):
+
+            @pl.when(jnp.logical_not(starts[way]))
+            def _(way=way):
+                @pl.when(ends[way])
+                def _():
+                    for copy in store_copies(way):
+                        copy.wait_recv()
+
+                for first in range(0, half, LANES):
+                    span = slice(first, first + LANES)
+                    w_tot[u, :, span] += value_of(wq_in[way, :, span], ws_in[way, :, span])
+
+        t_copy = remote(w_tot.at[u], w_tot.at[u], wt_sem, {"yr": sib})
+        t_copy.start()
+        chunk = 256
+        for first in range(0, units, chunk):
+            lane_of = lax.broadcasted_iota(jnp.int32, (LANES, chunk), 0)
+            hot = jnp.where(lane_of == (col_ref[:, first:first + chunk] & 127), 1.0, 0.0)
+            onel[first:first + chunk, :] = jnp.transpose(hot).astype(jnp.bfloat16)
+        t_copy.wait()
+        for h in range(2):
+            total = w_tot[h]
+            hi = total.astype(jnp.bfloat16)
+            w_hl[:rows, h * half:(h + 1) * half] = hi
+            w_hl[rows:, h * half:(h + 1) * half] = (total - hi.astype(jnp.float32)).astype(jnp.bfloat16)
+
+    base = (2 * b + u) * per
 
     def place(i, carry):
-        mask = jnp.where((col_ref[...] >> 7) == mine + i, 1.0, 0.0).astype(jnp.bfloat16)
+        mask = jnp.where((col_ref[...] >> 7) == base + i, 1.0, 0.0).astype(jnp.bfloat16)
         both = jnp.dot(w_hl[...] * mask, onel[...], preferred_element_type=jnp.float32)
         placed[i] = both[:rows] + both[rows:]
         return carry
 
-    lax.fori_loop(0, per, place, 0)
-
-    pair_copies[-1].wait()
-    for copies in sent:
-        for copy in copies:
-            copy.wait()
-
-    def finish(i, carry):
-        total = acc_ref[mine + i] + pair[nb - 1, i] + placed[i]
-        for j in range(len(order)):
-            total += value_of(q_in[j, i], s_in[j, pl.ds(i, 1)])
-        out_ref[:, pl.ds(pl.multiple_of(i * LANES, LANES), LANES)] = total
-        return carry
-
-    lax.fori_loop(0, per, finish, 0)
+    slots = max((nb - 2) * subs, 1)
+    quota = -(-per // slots)
+    done = 0
+    waited = set()
+    for k in range(nb - 1):
+        for t in (nb - 1 - k, k):
+            if t not in waited:
+                waited.add(t)
+                local_copies[t].wait()
+                pair_copies[t].wait()
+        for n in range(subs):
+            for way, t in ((0, nb - 1 - k), (1, k)):
+                sends = passes(way, t)
+                pl.when(sends & starts[way])(functools.partial(piece_send, way, t, n, False))
+                pl.when(sends & jnp.logical_not(starts[way]))(functools.partial(piece_send, way, t, n, True))
+            if k > 0 and done < per:
+                upto = min(per, done + quota)
+                lax.fori_loop(done, upto, place, 0)
+                done = upto
+        if k == 0:
+            collect()
+    if done < per:
+        lax.fori_loop(done, per, place, 0)
+    for t in sequence:
+        if t not in waited:
+            local_copies[t].wait()
+            pair_copies[t].wait()
+
+    def finish(t, ways):
+        for n in range(subs):
+            for way in ways:
+                for copy in piece_copies(way, t, n):
+                    copy.wait_recv()
+
+            def one(i, carry):
+                at = n * share + i
+                total = mine[t, at] + pair[t, at] + placed[at]
+                for way in ways:
+                    total += value_of(q_in[way, t, at], s_in[way, t, n, pl.ds(i, 1)])
+                out_ref[:, pl.ds(pl.multiple_of(at * LANES, LANES), LANES)] = total
+                return carry
+
+            lax.fori_loop(0, share, one, 0)
+
+    for t in range(nb):
+        ways = ([0] if t > 0 else []) + ([1] if t < nb - 1 else [])
+        pl.when(b == t)(functools.partial(finish, t, ways))
 
     for copy in small:
         copy.wait()
@@ -270,6 +338,18 @@
     for dc in range(nc):
         dots += e_in[dc]
     intercept_ref[...] = objective_ref[...] - jnp.transpose(dots)[:objective_ref.shape[0], :]
+
+    def settle(copies):
+        for copy in copies:
+            copy.wait_send()
+
+    for way in range(2):
+        pl.when(jnp.logical_not(ends[way]))(lambda way=way: settle(store_copies(way)))
+    for way in range(2):
+        for t in range(nb):
+            if (way == 0 and t > 0) or (way == 1 and t < nb - 1):
+                for n in range(subs):
+                    pl.when(passes(way, t))(lambda way=way, t=t, n=n: settle(piece_copies(way, t, n)))
 
 
 def local(nb, nc, price, avail, tile_ids, soc, link, retain, store_col, weight, capacity, objective):
@@ -325,10 +405,13 @@
     tail = jnp.broadcast_to(weight[:, weeks - 1][:, None, None], (years, 1, LANES))
     vmem = pl.BlockSpec(memory_space=pltpu.VMEM)
     dma = pltpu.SemaphoreType.DMA
+    subs = max(per // 8, 1)
     out, intercept = pl.pallas_call(
-        functools.partial(reduce_kernel, nb, nc),
+        functools.partial(reduce_kernel, nb, nc, subs),
         grid=(1,),
-        in_specs=[vmem, vmem, pl.BlockSpec((years, 1, rows, units), lambda g: (0, 0, 0, 0))] + [vmem] * 6,
+        in_specs=[pl.BlockSpec(memory_space=pl.ANY), vmem]
+        + [pl.BlockSpec((years, 1, rows, units), lambda g: (0, 0, 0, 0))]
+        + [vmem] * 6,
         out_specs=[vmem, vmem],
         out_shape=[
             jax.ShapeDtypeStruct((rows, piece), f32),
@@ -336,32 +419,34 @@
         ],
         scratch_shapes=[
             pltpu.VMEM((nb, per, rows, width), f32),
-            pltpu.VMEM((nb - 1, per, rows, width), jnp.int16),
-            pltpu.VMEM((nb - 1, per, width), f32),
-            pltpu.VMEM((nb - 1, per, rows, width), jnp.int16),
-            pltpu.VMEM((nb - 1, per, width), f32),
+            pltpu.VMEM((nb, per, rows, width), f32),
+            pltpu.VMEM((nb, per, rows, width), jnp.int16),
+            pltpu.VMEM((nb, subs, per // subs, width), f32),
+            pltpu.VMEM((2, nb, per, rows, width), jnp.int16),
+            pltpu.VMEM((2, nb, subs, per // subs, width), f32),
             pltpu.VMEM((years, 1, LANES), f32),
             pltpu.VMEM((max(nc - 1, 1), rows, LANES), f32),
             pltpu.VMEM((nc, rows, LANES), f32),
             pltpu.VMEM((2, rows, half), f32),
             pltpu.VMEM((rows, half), f32),
-            pltpu.VMEM((rows, half), jnp.int16),
-            pltpu.VMEM((1, half), f32),
-            pltpu.VMEM((nb - 1, rows, half), jnp.int16),
-            pltpu.VMEM((nb - 1, 1, half), f32),
+            pltpu.VMEM((2, rows, half), jnp.int16),
+            pltpu.VMEM((2, 1, half), f32),
+            pltpu.VMEM((2, rows, half), jnp.int16),
+            pltpu.VMEM((2, 1, half), f32),
             pltpu.VMEM((2, rows, half), f32),
             pltpu.VMEM((2 * rows, units), jnp.bfloat16),
             pltpu.VMEM((units, LANES), jnp.bfloat16),
             pltpu.VMEM((per, rows, width), f32),
+            dma((nb,)),
             dma((nb, 2)),
-            dma((nb - 1, 2)),
-            dma((nb - 1, 2)),
+            dma((2, nb, subs, 2)),
+            dma((2, nb, subs, 2)),
             dma((2,)),
             dma((max(nc - 1, 1), 2)),
             dma((nc, 2)),
             dma((2,)),
-            dma((nb - 1, 2)),
-            dma((nb - 1, 2)),
+            dma((2, 2)),
+            dma((2, 2)),
             dma((2,)),
         ],
         compiler_params=pltpu.CompilerParams(

time: 103 us -> 104 us (level)
  the two profiles are of different devices: /device:TPU:0 before, /device:TPU:20 now
where the time goes in v2:
time: 104 us
  Pallas kernels  94.5 us (91%)
  local copies, waits for them, and re-layouts  8.54 us (8%)
    pallas_call x1, Pallas kernels, local(): pl.pallas_call(functools.partial(reduce_kernel, nb, nc, subs), grid=(1,),...  77.6 us
    pallas_call x1, Pallas kernels, local(): pl.pallas_call(functools.partial(local_kernel, years, weeks), grid_spec=p...  16.9 us
    unnamed x3, local copies, waits for them, and re-layouts  5.31 us

profile of v2, /device:TPU:20, one launch (start us, length us, event | category | flops | bytes accessed | tf_op | source)
XLA Modules:
  0.0 103.7 jit_solution(182435979414287400)
XLA Ops:
  0.6 1.3 %reshape.28.ids_ref = s32[128]{0:T(128)} reshape(s32[4,2,16]{2,1,0:T(2,128)} %param.12) | data formatting | bytes 1024 | tf_op jit(solution)/shard_map/reshape | solution.py:403
  1.9 0.7 slice_bitcast_fusion
  2.6 0.7 broadcast_in_dim.11.tail_ref
  3.3 0.8 copy.14
  4.0 0.6 reshape.29.weight_ref
  4.6 16.9 %shard_map.113 = (f32[256,64,128]{2,1,0:T(8,128)}, f32[64,2048]{1,0:T(8,128)}, f32[64,128]{1,0:T(8,128)}, f32[64,128]{1,0:T(8,128)}) custom-call(s32[128]{0:T(128)} %reshape.28.ids_ref, f32[8]{0:T(128)} %reshape.29.weight_ref, bf16[4,2,64,168]{3,2,1,0:T(8,128)(2,1)} %price_ref.1, bf16[4,2,16,168,128]{4,3,2,1,0:T(8,128)(2,1)} %avail_ref.1, ...), custom_call_target="tpu_custom_call" | custom-call | tf_op jit(solution)/shard_map/pallas_call | solution.py:374
  21.5 77.6 %shard_map.114 = (f32[64,4096]{1,0:T(8,128)}, f32[8,64]{1,0:T(8,128)}) custom-call(f32[256,64,128]{2,1,0:T(8,128)} %get-tuple-element.8.acc_ref, f32[64,2048]{1,0:T(8,128)} %get-tuple-element.9.wsum_ref, bf16[4,2,64,2048]{3,2,1,0:T(8,128)(2,1)} %first_ref.1, f32[1,2048]{1,0:T(1,128)} %bitcast.11, f32[4,1,128]{2,1,0:T(1,128)} %broadcast_in_dim.11.tail_ref, ...), custom_call_target="tpu_custom_call" | custom-call | tf_op jit(solution)/shard_map/pallas_call | solution.py:409
  99.1 3.3 %copy.15 = f32[64,1,4096]{2,1,0:T(1,128)} copy(f32[64,1,4096]{2,0,1:T(8,128)} %bitcast.8) | data formatting | bytes 2097152
  102.4 1.3 %copy.17 = f32[4,2,64]{2,1,0:T(2,128)} copy(f32[4,2,64]{2,1,0:T(2,128)} %bitcast.15) | data formatting | bytes 4096

commit v3 on v1

--- a/solution.py
+++ b/solution.py
@@ -54,13 +54,13 @@
             found = jnp.where(lane_of == (col & 127), found, 0.0)
             caps_ref[:, first:first + chunk] = jnp.sum(found, axis=0, keepdims=True)
 
-    here = weight_ref[step]
-    inside = lax.rem(step, weeks)
-    before = jnp.where(inside > 0, weight_ref[jnp.maximum(step - 1, 0)], 0.0)
+    year, inside = step // weeks, lax.rem(step, weeks)
+    here = weight_ref[year, inside]
+    before = jnp.where(inside > 0, weight_ref[year, jnp.maximum(inside - 1, 0)], 0.0)
     duals = price_ref[0, 0]
     tile_dots = jnp.zeros((rows, LANES), jnp.float32)
     for k in range(tiles):
-        index = ids_ref[step * tiles + k]
+        index = ids_ref[year, inside, k]
         cut = jnp.dot(duals, avail_ref[0, 0, k], preferred_element_type=jnp.float32)
         tile_dots += cut * cap_ref[index]
         acc_ref[index] += here * cut
@@ -319,8 +319,8 @@
             jax.ShapeDtypeStruct((rows, LANES), f32),
             jax.ShapeDtypeStruct((rows, LANES), f32),
         ],
-        compiler_params=pltpu.CompilerParams(vmem_limit_bytes=VMEM_LIMIT),
-    )(tile_ids.reshape(-1), weight.reshape(-1), price, avail, soc, link, retain2, col2, capacity.reshape(tile_count, 1, width))
+        compiler_params=pltpu.CompilerParams(vmem_limit_bytes=60 * 1024 * 1024),
+    )(tile_ids, weight, price, avail, soc, link, retain2, col2, capacity.reshape(tile_count, 1, width))
 
     tail = jnp.broadcast_to(weight[:, weeks - 1][:, None, None], (years, 1, LANES))
     vmem = pl.BlockSpec(memory_space=pltpu.VMEM)

time: 103 us -> 100 us (0.971)
  local copies, waits for them, and re-layouts: 11.5 us -> 7.45 us
  Pallas kernels: 89.9 us -> 91.4 us
    unnamed x19 -> x17, local copies, waits for them, and re-layouts: 9.84 us -> 6.55 us
    pallas_call x1, Pallas kernels: 15.5 us -> 17 us  [local(): pl.pallas_call(functools.partial(local_kernel, years, weeks), grid_spec=p...]
where the time goes in v3:
time: 100 us; the launch traced here: 99.5 us
  Pallas kernels  91.4 us (91%)
  local copies, waits for them, and re-layouts  7.45 us (7%)
    pallas_call x1, Pallas kernels, local(): pl.pallas_call(functools.partial(reduce_kernel, nb, nc), grid=(1,), in_sp...  74.4 us
    pallas_call x1, Pallas kernels, local(): pl.pallas_call(functools.partial(local_kernel, years, weeks), grid_spec=p...  17 us
    unnamed x17, local copies, waits for them, and re-layouts  6.55 us

profile of v3, /device:TPU:0, one launch (start us, length us, event | category | flops | bytes accessed | tf_op | source)
XLA Modules:
  0.0 99.5 jit_solution(8796739961284308233)
XLA Ops:
  0.6 0.0 copy-start
  0.6 0.0 copy-start.6
  0.7 0.0 copy-start.5
  0.7 0.0 copy-start.4
  0.7 0.8 slice_bitcast_fusion
  1.5 0.1 broadcast_in_dim.11.tail_ref
  1.6 1.3 %copy.12.weight_ref = f32[4,2]{1,0:T(4,128)} copy(f32[4,2]{0,1:T(2,128)} %param.17) | data formatting | bytes 64 | tf_op args[7]
  2.9 17.0 %shard_map.113 = (f32[256,64,128]{2,1,0:T(8,128)}, f32[64,2048]{1,0:T(8,128)}, f32[64,128]{1,0:T(8,128)}, f32[64,128]{1,0:T(8,128)}) custom-call(s32[4,2,16]{2,1,0:T(2,128)} %ids_ref.1, f32[4,2]{1,0:T(4,128)} %copy.12.weight_ref, bf16[4,2,64,168]{3,2,1,0:T(8,128)(2,1)} %price_ref.1, bf16[4,2,16,168,128]{4,3,2,1,0:T(8,128)(2,1)} %avail_ref.1, ...), custom_call_target="tpu_custom_call" | custom-call | tf_op jit(solution)/shard_map/pallas_call | solution.py:294
  19.9 0.0 copy-done
  19.9 0.0 copy-done.6
  19.9 0.0 copy-done.5
  19.9 0.0 copy-done.4
  19.9 0.0 copy-start.1
  19.9 1.0 %copy-done.1 = f32[64,2048]{1,0:T(8,128)S(1)} copy-done((f32[64,2048]{1,0:T(8,128)S(1)}, f32[64,2048]{1,0:T(8,128)}, u32[]{:S(2)}) %copy-start.1) | copy-done | bytes 524312
  21.0 0.0 copy-start.2
  21.0 0.8 copy-done.2
  21.7 0.0 copy-start.3
  21.7 0.8 copy-done.3
  22.5 74.4 %shard_map.114 = (f32[64,4096]{1,0:T(8,128)S(1)}, f32[8,64]{1,0:T(8,128)S(1)}) custom-call(f32[256,64,128]{2,1,0:T(8,128)} %get-tuple-element.8.acc_ref, f32[64,2048]{1,0:T(8,128)S(1)} %copy-done.1, bf16[4,2,64,2048]{3,2,1,0:T(8,128)(2,1)S(1)} %copy-done, f32[1,2048]{1,0:T(1,128)S(1)} %bitcast.10, f32[4,1,128]{2,1,0:T(1,128)S(1)} %broadcast_in_dim.11.tail_ref, ...), custom_call_target="tpu_custom_call" | custom-call | tf_op jit(solution)/shard_map/pallas_call | solution.py:328
  96.9 2.0 %copy.13 = f32[64,1,4096]{2,1,0:T(1,128)} copy(f32[64,1,4096]{2,0,1:T(8,128)S(1)} %bitcast.8) | data formatting | bytes 2097152
  98.9 0.6 copy.15
Async XLA Ops:
  0.6 19.3 %copy-start = (bf16[4,2,64,2048]{3,2,1,0:T(8,128)(2,1)S(1)}, bf16[4,2,64,2048]{3,2,1,0:T(8,128)(2,1)}, u32[]{:S(2)}) copy-start(bf16[4,2,64,2048]{3,2,1,0:T(8,128)(2,1)} %first_ref.1) | copy-start | bytes 6291460
  0.6 19.2 %copy-start.6 = (f32[4,2,64]{2,1,0:T(2,128)S(1)}, f32[4,2,64]{2,1,0:T(2,128)}, u32[]{:S(2)}) copy-start(f32[4,2,64]{2,1,0:T(2,128)} %param.19) | copy-start | bytes 6148
  0.7 19.2 %copy-start.5 = (s32[2048]{0:T(1024)S(1)}, s32[2048]{0:T(1024)}, u32[]{:S(2)}) copy-start(s32[2048]{0:T(1024)} %param.16) | copy-start | bytes 24580
  0.7 19.2 %copy-start.4 = (f32[2048]{0:T(1024)S(1)}, f32[2048]{0:T(1024)}, u32[]{:S(2)}) copy-start(f32[2048]{0:T(1024)} %param.15) | copy-start | bytes 24580
  19.9 1.0 %copy-start.1 = (f32[64,2048]{1,0:T(8,128)S(1)}, f32[64,2048]{1,0:T(8,128)}, u32[]{:S(2)}) copy-start(f32[64,2048]{1,0:T(8,128)} %get-tuple-element.9.wsum_ref) | copy-start | bytes 1572868
  21.0 0.8 copy-start.2
  21.7 0.8 copy-start.3
